TPU v7x, 32 devices: a whole 2x2x4 slice. The times are simulated.
32 devices in a mesh: dp: 2 (over core), head: 2 (over x), ctx: 8 (over z, y).
Axes of the slice: x: 2, y: 2, z: 4, core: 2. Of those that a mesh axis runs over, the one named last changes fastest.
Arguments:
- query_states: bfloat16 [2, 8192, 32, 128], P('dp', 'ctx', 'head'), may hold values from -6 to 6
- key_states: bfloat16 [2, 8192, 8, 128], P('dp', 'ctx', 'head'), may hold values from -6 to 6
- value_states: bfloat16 [2, 8192, 8, 128], P('dp', 'ctx', 'head'), may hold values from -12 to 12
- gate_values: float32 [32], P('head'), may hold values from 0.1 to 0.9
- head_flags: int32 [32], P('head'), may hold values from 0 to 1, as said below
- output_grad: bfloat16 [2, 8192, 32, 128], P('dp', 'ctx', 'head'), may hold values from -16 to 16
Outputs:
- blended: bfloat16 [2, 8192, 32, 128], P('dp', 'ctx', 'head')
- gate_grad: float32 [32], replicated
Inputs may be any that keep to these rules, and one draw needn't show every extreme that they name: `head_flags`: exactly 1 of the 4 query heads of each key-value head have flag 1.
All inputs are finite; a program needn't handle non-finite values.
Results may differ from a plain program's by a relative error of at most 0.005.
Values may be sent and summed in bfloat16 or wider, within the bound.
A program may use at most 128 MiB of HBM per device.

v0:
```python
import math

import jax
import jax.numpy as jnp
from jax import lax
from jax.sharding import PartitionSpec as P

RET = 1
SINK = 64
WINDOW = 2048


def from_behind(block, axis, distance):
    devices = range(lax.axis_size(axis))
    route = [(i - distance, i) for i in devices if i - distance in devices]
    return lax.ppermute(block, axis, route)


def empty_state(row_count, groups, heads, width):
    return (
        jnp.full((row_count, groups, heads), -jnp.inf, jnp.float32),
        jnp.zeros((row_count, groups, heads), jnp.float32),
        jnp.zeros((row_count, groups, heads, width), jnp.float32),
    )


def block_update(carried, query_block, key_rows, value_rows, allowed):
    running_max, running_sum, running_acc = carried
    scaling = 1.0 / math.sqrt(query_block.shape[-1])
    scores = (
        jnp.einsum("rgeh,kgh->rgek", query_block, key_rows, preferred_element_type=jnp.float32)
        * scaling
    )
    visible = allowed[:, None, None, :]
    scores = jnp.where(visible, scores, -jnp.inf)
    newest = jnp.maximum(running_max, jnp.max(scores, axis=-1))
    anchor = jnp.where(newest == -jnp.inf, 0.0, newest)
    factor = jnp.exp(running_max - anchor)
    weights = jnp.where(visible, jnp.exp(scores - anchor[..., None]), 0.0)
    running_sum = running_sum * factor + jnp.sum(weights, axis=-1)
    update = jnp.einsum(
        "rgek,kgh->rgeh",
        weights.astype(jnp.bfloat16),
        value_rows,
        preferred_element_type=jnp.float32,
    )
    running_acc = running_acc * factor[..., None] + update
    return (newest, running_sum, running_acc)


def sweep_blocks(carried, queries, positions, key_rows, value_rows, key_first, needed, allowed_fn):
    row_count = queries.shape[0]
    key_count = key_rows.shape[0]
    row_block = math.gcd(row_count, 512)
    key_block = math.gcd(key_count, 512)
    key_steps = key_count // key_block
    total_steps = row_count // row_block * key_steps

    def visit_block(counter, current):
        row_at = counter // key_steps * row_block
        key_at = counter % key_steps * key_block
        row_pos = lax.dynamic_slice_in_dim(positions, row_at, row_block)
        key_pos = key_first + key_at + jnp.arange(key_block, dtype=jnp.int32)

        def compute(present):
            portion = tuple(
                (lax.dynamic_slice_in_dim(member, row_at, row_block) for member in present)
            )
            renewed = block_update(
                portion,
                lax.dynamic_slice_in_dim(queries, row_at, row_block),
                lax.dynamic_slice_in_dim(key_rows, key_at, key_block),
                lax.dynamic_slice_in_dim(value_rows, key_at, key_block),
                allowed_fn(row_pos[:, None], key_pos[None, :]),
            )
            return tuple(
                (
                    lax.dynamic_update_slice_in_dim(member, fresh_part, row_at, 0)
                    for member, fresh_part in zip(present, renewed)
                )
            )

        def unchanged(present):
            return present

        return lax.cond(
            needed(row_pos[0], row_pos[row_block - 1], key_pos[0], key_pos[key_block - 1]),
            compute,
            unchanged,
            current,
        )

    return lax.fori_loop(0, total_steps, visit_block, carried)


def causal_needed(row_low, row_high, key_low, key_high):
    return key_low <= row_high


def causal_allowed(row_pos, key_pos):
    return key_pos <= row_pos


def window_needed(row_low, row_high, key_low, key_high):
    return (key_low <= row_high) & (key_high > row_low - WINDOW)


def window_allowed(row_pos, key_pos):
    return (key_pos >= 0) & (key_pos <= row_pos) & (row_pos - key_pos < WINDOW)


def sinks_needed(row_low, row_high, key_low, key_high):
    return (key_low < SINK) & (row_high - key_low >= WINDOW)


def sinks_allowed(row_pos, key_pos):
    return (key_pos < SINK) & (key_pos <= row_pos) & (row_pos - key_pos >= WINDOW)


def on_device(query_states, key_states, value_states, gate_values, head_flags, output_grad):
    tok_rows = query_states.shape[1]
    groups = key_states.shape[2]
    head_dim = key_states.shape[3]
    per_group = query_states.shape[2] // groups
    ctx_count = lax.axis_size("ctx")
    ctx_index = lax.axis_index("ctx")
    queries = query_states[0].reshape(tok_rows, groups, per_group, head_dim)
    stacked = jnp.stack([key_states[0], value_states[0]])
    marked = head_flags.reshape(groups, per_group)
    ordinal = jnp.cumsum(marked, axis=1) - 1
    slot_ids = jnp.arange(RET, dtype=jnp.int32)
    picker = ((marked[:, None, :] == 1) & (ordinal[:, None, :] == slot_ids[None, :, None])).astype(
        jnp.float32
    )
    chosen = jnp.einsum(
        "gre,tgeh->tgrh", picker.astype(jnp.bfloat16), queries, preferred_element_type=jnp.float32
    ).astype(jnp.bfloat16)
    own_pos = ctx_index * tok_rows + jnp.arange(tok_rows, dtype=jnp.int32)
    full_state = empty_state(tok_rows, groups, RET, head_dim)
    near_state = empty_state(tok_rows, groups, per_group, head_dim)
    portion = lax.all_gather(stacked, "ctx", axis=1, tiled=True)
    start = jnp.int32(0)
    full_now = sweep_blocks(
        full_state, chosen, own_pos, portion[0], portion[1], start, causal_needed, causal_allowed
    )
    head_rows = min(SINK, portion.shape[1])
    sink_part = portion[:, :head_rows]

    def with_sinks(present):
        return sweep_blocks(
            present,
            queries,
            own_pos,
            sink_part[0],
            sink_part[1],
            start,
            sinks_needed,
            sinks_allowed,
        )

    def without_sinks(present):
        return present

    near_now = lax.cond(start < SINK, with_sinks, without_sinks, near_state)
    near_state = near_now
    reach_depth = min((WINDOW - 1) // tok_rows + 1, ctx_count - 1)
    earlier = [from_behind(stacked, "ctx", distance) for distance in range(reach_depth, 0, -1)]
    near_keys = jnp.concatenate(earlier + [stacked], axis=1)
    near_state = sweep_blocks(
        near_state,
        queries,
        own_pos,
        near_keys[0],
        near_keys[1],
        (ctx_index - reach_depth) * tok_rows,
        window_needed,
        window_allowed,
    )
    full_out = full_now[2] / full_now[1][..., None]
    near_out = near_state[2] / near_state[1][..., None]
    full_heads = jnp.einsum("gre,tgrh->tgeh", picker, full_out, precision=lax.Precision.HIGHEST)
    gate_cols = gate_values.reshape(groups, per_group)[None, :, :, None]
    retrieval = (marked == 1)[None, :, :, None]
    mixed = jnp.where(retrieval, gate_cols * full_heads + (1.0 - gate_cols) * near_out, near_out)
    blended = mixed.astype(jnp.bfloat16).reshape(1, tok_rows, groups * per_group, head_dim)
    grad_rows = output_grad[0].reshape(tok_rows, groups, per_group, head_dim).astype(jnp.float32)
    local_terms = jnp.sum(grad_rows * (full_heads - near_out), axis=(0, 3)) * marked.astype(
        jnp.float32
    )
    heads_dev = groups * per_group
    padded = lax.dynamic_update_slice_in_dim(
        jnp.zeros((heads_dev * lax.axis_size("head"),), jnp.float32),
        local_terms.reshape(heads_dev),
        lax.axis_index("head") * heads_dev,
        0,
    )
    totals = lax.psum(padded, ("dp", "head", "ctx"))
    normalizer = 1.0 / math.sqrt(
        lax.axis_size("dp") * query_states.shape[0] * tok_rows * ctx_count * head_dim
    )
    return (blended, totals * normalizer)


def solution(mesh):
    return jax.shard_map(
        on_device,
        mesh=mesh,
        in_specs=(
            P("dp", "ctx", "head", None),
            P("dp", "ctx", "head", None),
            P("dp", "ctx", "head", None),
            P("head"),
            P("head"),
            P("dp", "ctx", "head", None),
        ),
        out_specs=(P("dp", "ctx", "head", None), P()),
        check_vma=False,
    )
```

profile of v0, /device:TPU:0, one launch (start us, length us, event | category | flops | bytes accessed | tf_op | source)
XLA Modules:
  0.0 1334.1 jit_solution(6311625339541324316)
XLA Ops:
  42.2 41.9 %collective-permute-done.1 = bf16[2,1024,4,128]{3,1,2,0:T(8,128)(2,1)} collective-permute-done((bf16[2,1024,4,128]{3,1,2,0:T(8,128)(2,1)}, bf16[2,1024,4,128]{3,1,2,0:T(8,128)(2,1)}, u32[]{:S(2)}, u32[]{:S(2)}) %collective-permute-start.1) | collective-permute-done | bytes 2097184 | tf_op jit(solution)/shard_map/ppermute | solution.py:16
  84.1 21.8 %collective-permute-done = bf16[2,1024,4,128]{3,1,2,0:T(8,128)(2,1)} collective-permute-done((bf16[2,1024,4,128]{3,1,2,0:T(8,128)(2,1)}, bf16[2,1024,4,128]{3,1,2,0:T(8,128)(2,1)}, u32[]{:S(2)}, u32[]{:S(2)}) %collective-permute-start) | collective-permute-done | bytes 2097184 | tf_op jit(solution)/shard_map/ppermute | solution.py:16
  116.7 190.5 %all-gather.2.cloned.1.call-done = bf16[2,8192,4,128]{3,1,2,0:T(8,128)(2,1)} async-done(((bf16[2,1024,4,128]{3,1,2,0:T(8,128)(2,1)}), bf16[2,8192,4,128]{3,1,2,0:T(8,128)(2,1)}) %all-gather.2.cloned.1.call-update) | async-done | bytes 16777232 | tf_op jit(solution)/shard_map/all_gather | solution.py:141
  307.1 11.4 slice_bitcast_fusion
  318.5 11.6 copy.24
  331.7 118.5 %while.58 = (s32[]{:T(128)}, f32[1024,4,1]{0,1,2:T(4,128)S(1)}, f32[1024,4,1]{0,1,2:T(4,128)S(1)}, f32[1024,4,1,128]{0,3,1,2:T(8,128)}, s32[1024]{0:T(1024)S(1)}...) while((s32[]{:T(128)}, f32[1024,4,1]{0,1,2:T(4,128)S(1)}, ...), condition=%wide.region_6.7_spmd, body=%wide.region_1.6_spmd.sunk | while | flops 551307776 | bytes 19573344 | solution.py:93
  334.2 13.0 conditional.6
  388.0 12.0 conditional.6
  402.5 12.0 conditional.6
  467.1 433.6 %while.60 = (s32[]{:T(128)}, f32[1024,4,4]{0,2,1:T(4,128)S(1)}, f32[1024,4,4]{0,2,1:T(4,128)S(1)}, f32[1024,4,4,128]{0,3,2,1:T(8,128)}, s32[]{:T(128)}, /*index=...) while((s32[]{:T(128)}, f32[1024,4,4]{0,2,1:T(4,128)S(1)}, ...), condition=%wide.region_18.19_spmd, body=%wide.region_13.18_spmd.sunk | while | flops 2205467648 | bytes 71939728 | solution.py:93
  470.4 40.0 %conditional.8 = ((f32[1024,4,4]{0,2,1:T(4,128)S(1)}, f32[1024,4,4]{0,2,1:T(4,128)S(1)}, f32[1024,4,4,128]{0,3,2,1:T(8,128)})) conditional(s32[]{:T(128)} %bitcast.153, (f32[1024,4,4]{0,2,1:T(4,128)S(1)}, f32[1024,4,4]{0,2,1:T(4,128)S(1)}, f32[1024,4,4,128]{0,3,2,1:T(8,128)}) %tuple.166, (s32[]{:T(128)}, f32[1024,4,4]{0,2,1:T(4,128)S(1)}, ...), branch_computations={%region_14.14_spmd, %region_15.17_spmd} | conditional | flops 2205467136 | bytes 71933064 | solution.py:86
  480.1 9.3 bitcast_add_fusion.2
  490.1 20.3 %dynamic_update_slice.31 = f32[1024,4,4,128]{0,3,2,1:T(8,128)} dynamic-update-slice(f32[1024,4,4,128]{0,3,2,1:T(8,128)} %get-tuple-element.818, f32[512,4,4,128]{0,3,2,1:T(8,128)} %bitcast_add_fusion.2, s32[]{:T(128)S(6)} %select_n.182, s32[]{:T(128)} %constant.327.clone, s32[]{:T(128)} %constant.327.clone, s32[]{:T(128)} %constant.327.clone) | dynamic-update-slice | bytes 8388612 | tf_op jit(solution)/shard_map/while/body/eval_jaxpr/cond/branch_1_fun/dynamic_update_slice | solution.py:78
  513.7 40.0 %conditional.8 = ((f32[1024,4,4]{0,2,1:T(4,128)S(1)}, f32[1024,4,4]{0,2,1:T(4,128)S(1)}, f32[1024,4,4,128]{0,3,2,1:T(8,128)})) conditional(s32[]{:T(128)} %bitcast.153, (f32[1024,4,4]{0,2,1:T(4,128)S(1)}, f32[1024,4,4]{0,2,1:T(4,128)S(1)}, f32[1024,4,4,128]{0,3,2,1:T(8,128)}) %tuple.166, (s32[]{:T(128)}, f32[1024,4,4]{0,2,1:T(4,128)S(1)}, ...), branch_computations={%region_14.14_spmd, %region_15.17_spmd} | conditional | flops 2205467136 | bytes 71933064 | solution.py:86
  533.3 20.3 %dynamic_update_slice.31 = f32[1024,4,4,128]{0,3,2,1:T(8,128)} dynamic-update-slice(f32[1024,4,4,128]{0,3,2,1:T(8,128)} %get-tuple-element.818, f32[512,4,4,128]{0,3,2,1:T(8,128)} %bitcast_add_fusion.2, s32[]{:T(128)S(6)} %select_n.182, s32[]{:T(128)} %constant.327.clone, s32[]{:T(128)} %constant.327.clone, s32[]{:T(128)} %constant.327.clone) | dynamic-update-slice | bytes 8388612 | tf_op jit(solution)/shard_map/while/body/eval_jaxpr/cond/branch_1_fun/dynamic_update_slice | solution.py:78
  556.9 40.0 %conditional.8 = ((f32[1024,4,4]{0,2,1:T(4,128)S(1)}, f32[1024,4,4]{0,2,1:T(4,128)S(1)}, f32[1024,4,4,128]{0,3,2,1:T(8,128)})) conditional(s32[]{:T(128)} %bitcast.153, (f32[1024,4,4]{0,2,1:T(4,128)S(1)}, f32[1024,4,4]{0,2,1:T(4,128)S(1)}, f32[1024,4,4,128]{0,3,2,1:T(8,128)}) %tuple.166, (s32[]{:T(128)}, f32[1024,4,4]{0,2,1:T(4,128)S(1)}, ...), branch_computations={%region_14.14_spmd, %region_15.17_spmd} | conditional | flops 2205467136 | bytes 71933064 | solution.py:86
  576.6 20.3 %dynamic_update_slice.31 = f32[1024,4,4,128]{0,3,2,1:T(8,128)} dynamic-update-slice(f32[1024,4,4,128]{0,3,2,1:T(8,128)} %get-tuple-element.818, f32[512,4,4,128]{0,3,2,1:T(8,128)} %bitcast_add_fusion.2, s32[]{:T(128)S(6)} %select_n.182, s32[]{:T(128)} %constant.327.clone, s32[]{:T(128)} %constant.327.clone, s32[]{:T(128)} %constant.327.clone) | dynamic-update-slice | bytes 8388612 | tf_op jit(solution)/shard_map/while/body/eval_jaxpr/cond/branch_1_fun/dynamic_update_slice | solution.py:78
  600.2 40.0 %conditional.8 = ((f32[1024,4,4]{0,2,1:T(4,128)S(1)}, f32[1024,4,4]{0,2,1:T(4,128)S(1)}, f32[1024,4,4,128]{0,3,2,1:T(8,128)})) conditional(s32[]{:T(128)} %bitcast.153, (f32[1024,4,4]{0,2,1:T(4,128)S(1)}, f32[1024,4,4]{0,2,1:T(4,128)S(1)}, f32[1024,4,4,128]{0,3,2,1:T(8,128)}) %tuple.166, (s32[]{:T(128)}, f32[1024,4,4]{0,2,1:T(4,128)S(1)}, ...), branch_computations={%region_14.14_spmd, %region_15.17_spmd} | conditional | flops 2205467136 | bytes 71933064 | solution.py:86
  619.8 20.3 %dynamic_update_slice.31 = f32[1024,4,4,128]{0,3,2,1:T(8,128)} dynamic-update-slice(f32[1024,4,4,128]{0,3,2,1:T(8,128)} %get-tuple-element.818, f32[512,4,4,128]{0,3,2,1:T(8,128)} %bitcast_add_fusion.2, s32[]{:T(128)S(6)} %select_n.182, s32[]{:T(128)} %constant.327.clone, s32[]{:T(128)} %constant.327.clone, s32[]{:T(128)} %constant.327.clone) | dynamic-update-slice | bytes 8388612 | tf_op jit(solution)/shard_map/while/body/eval_jaxpr/cond/branch_1_fun/dynamic_update_slice | solution.py:78
  643.4 40.0 %conditional.8 = ((f32[1024,4,4]{0,2,1:T(4,128)S(1)}, f32[1024,4,4]{0,2,1:T(4,128)S(1)}, f32[1024,4,4,128]{0,3,2,1:T(8,128)})) conditional(s32[]{:T(128)} %bitcast.153, (f32[1024,4,4]{0,2,1:T(4,128)S(1)}, f32[1024,4,4]{0,2,1:T(4,128)S(1)}, f32[1024,4,4,128]{0,3,2,1:T(8,128)}) %tuple.166, (s32[]{:T(128)}, f32[1024,4,4]{0,2,1:T(4,128)S(1)}, ...), branch_computations={%region_14.14_spmd, %region_15.17_spmd} | conditional | flops 2205467136 | bytes 71933064 | solution.py:86
  663.1 20.3 %dynamic_update_slice.31 = f32[1024,4,4,128]{0,3,2,1:T(8,128)} dynamic-update-slice(f32[1024,4,4,128]{0,3,2,1:T(8,128)} %get-tuple-element.818, f32[512,4,4,128]{0,3,2,1:T(8,128)} %bitcast_add_fusion.2, s32[]{:T(128)S(6)} %select_n.182, s32[]{:T(128)} %constant.327.clone, s32[]{:T(128)} %constant.327.clone, s32[]{:T(128)} %constant.327.clone) | dynamic-update-slice | bytes 8388612 | tf_op jit(solution)/shard_map/while/body/eval_jaxpr/cond/branch_1_fun/dynamic_update_slice | solution.py:78
  693.4 38.9 %conditional.8 = ((f32[1024,4,4]{0,2,1:T(4,128)S(1)}, f32[1024,4,4]{0,2,1:T(4,128)S(1)}, f32[1024,4,4,128]{0,3,2,1:T(8,128)})) conditional(s32[]{:T(128)} %bitcast.153, (f32[1024,4,4]{0,2,1:T(4,128)S(1)}, f32[1024,4,4]{0,2,1:T(4,128)S(1)}, f32[1024,4,4,128]{0,3,2,1:T(8,128)}) %tuple.166, (s32[]{:T(128)}, f32[1024,4,4]{0,2,1:T(4,128)S(1)}, ...), branch_computations={%region_14.14_spmd, %region_15.17_spmd} | conditional | flops 2205467136 | bytes 71933064 | solution.py:86
  712.8 19.5 %dynamic_update_slice.31 = f32[1024,4,4,128]{0,3,2,1:T(8,128)} dynamic-update-slice(f32[1024,4,4,128]{0,3,2,1:T(8,128)} %get-tuple-element.818, f32[512,4,4,128]{0,3,2,1:T(8,128)} %bitcast_add_fusion.2, s32[]{:T(128)S(6)} %select_n.182, s32[]{:T(128)} %constant.327.clone, s32[]{:T(128)} %constant.327.clone, s32[]{:T(128)} %constant.327.clone) | dynamic-update-slice | bytes 8388612 | tf_op jit(solution)/shard_map/while/body/eval_jaxpr/cond/branch_1_fun/dynamic_update_slice | solution.py:78
  735.5 38.9 %conditional.8 = ((f32[1024,4,4]{0,2,1:T(4,128)S(1)}, f32[1024,4,4]{0,2,1:T(4,128)S(1)}, f32[1024,4,4,128]{0,3,2,1:T(8,128)})) conditional(s32[]{:T(128)} %bitcast.153, (f32[1024,4,4]{0,2,1:T(4,128)S(1)}, f32[1024,4,4]{0,2,1:T(4,128)S(1)}, f32[1024,4,4,128]{0,3,2,1:T(8,128)}) %tuple.166, (s32[]{:T(128)}, f32[1024,4,4]{0,2,1:T(4,128)S(1)}, ...), branch_computations={%region_14.14_spmd, %region_15.17_spmd} | conditional | flops 2205467136 | bytes 71933064 | solution.py:86
  754.9 19.5 %dynamic_update_slice.31 = f32[1024,4,4,128]{0,3,2,1:T(8,128)} dynamic-update-slice(f32[1024,4,4,128]{0,3,2,1:T(8,128)} %get-tuple-element.818, f32[512,4,4,128]{0,3,2,1:T(8,128)} %bitcast_add_fusion.2, s32[]{:T(128)S(6)} %select_n.182, s32[]{:T(128)} %constant.327.clone, s32[]{:T(128)} %constant.327.clone, s32[]{:T(128)} %constant.327.clone) | dynamic-update-slice | bytes 8388612 | tf_op jit(solution)/shard_map/while/body/eval_jaxpr/cond/branch_1_fun/dynamic_update_slice | solution.py:78
  777.6 38.9 %conditional.8 = ((f32[1024,4,4]{0,2,1:T(4,128)S(1)}, f32[1024,4,4]{0,2,1:T(4,128)S(1)}, f32[1024,4,4,128]{0,3,2,1:T(8,128)})) conditional(s32[]{:T(128)} %bitcast.153, (f32[1024,4,4]{0,2,1:T(4,128)S(1)}, f32[1024,4,4]{0,2,1:T(4,128)S(1)}, f32[1024,4,4,128]{0,3,2,1:T(8,128)}) %tuple.166, (s32[]{:T(128)}, f32[1024,4,4]{0,2,1:T(4,128)S(1)}, ...), branch_computations={%region_14.14_spmd, %region_15.17_spmd} | conditional | flops 2205467136 | bytes 71933064 | solution.py:86
  797.0 19.5 %dynamic_update_slice.31 = f32[1024,4,4,128]{0,3,2,1:T(8,128)} dynamic-update-slice(f32[1024,4,4,128]{0,3,2,1:T(8,128)} %get-tuple-element.818, f32[512,4,4,128]{0,3,2,1:T(8,128)} %bitcast_add_fusion.2, s32[]{:T(128)S(6)} %select_n.182, s32[]{:T(128)} %constant.327.clone, s32[]{:T(128)} %constant.327.clone, s32[]{:T(128)} %constant.327.clone) | dynamic-update-slice | bytes 8388612 | tf_op jit(solution)/shard_map/while/body/eval_jaxpr/cond/branch_1_fun/dynamic_update_slice | solution.py:78
  819.8 38.9 %conditional.8 = ((f32[1024,4,4]{0,2,1:T(4,128)S(1)}, f32[1024,4,4]{0,2,1:T(4,128)S(1)}, f32[1024,4,4,128]{0,3,2,1:T(8,128)})) conditional(s32[]{:T(128)} %bitcast.153, (f32[1024,4,4]{0,2,1:T(4,128)S(1)}, f32[1024,4,4]{0,2,1:T(4,128)S(1)}, f32[1024,4,4,128]{0,3,2,1:T(8,128)}) %tuple.166, (s32[]{:T(128)}, f32[1024,4,4]{0,2,1:T(4,128)S(1)}, ...), branch_computations={%region_14.14_spmd, %region_15.17_spmd} | conditional | flops 2205467136 | bytes 71933064 | solution.py:86
  839.2 19.5 %dynamic_update_slice.31 = f32[1024,4,4,128]{0,3,2,1:T(8,128)} dynamic-update-slice(f32[1024,4,4,128]{0,3,2,1:T(8,128)} %get-tuple-element.818, f32[512,4,4,128]{0,3,2,1:T(8,128)} %bitcast_add_fusion.2, s32[]{:T(128)S(6)} %select_n.182, s32[]{:T(128)} %constant.327.clone, s32[]{:T(128)} %constant.327.clone, s32[]{:T(128)} %constant.327.clone) | dynamic-update-slice | bytes 8388612 | tf_op jit(solution)/shard_map/while/body/eval_jaxpr/cond/branch_1_fun/dynamic_update_slice | solution.py:78
  861.9 38.9 %conditional.8 = ((f32[1024,4,4]{0,2,1:T(4,128)S(1)}, f32[1024,4,4]{0,2,1:T(4,128)S(1)}, f32[1024,4,4,128]{0,3,2,1:T(8,128)})) conditional(s32[]{:T(128)} %bitcast.153, (f32[1024,4,4]{0,2,1:T(4,128)S(1)}, f32[1024,4,4]{0,2,1:T(4,128)S(1)}, f32[1024,4,4,128]{0,3,2,1:T(8,128)}) %tuple.166, (s32[]{:T(128)}, f32[1024,4,4]{0,2,1:T(4,128)S(1)}, ...), branch_computations={%region_14.14_spmd, %region_15.17_spmd} | conditional | flops 2205467136 | bytes 71933064 | solution.py:86
  881.3 19.5 %dynamic_update_slice.31 = f32[1024,4,4,128]{0,3,2,1:T(8,128)} dynamic-update-slice(f32[1024,4,4,128]{0,3,2,1:T(8,128)} %get-tuple-element.818, f32[512,4,4,128]{0,3,2,1:T(8,128)} %bitcast_add_fusion.2, s32[]{:T(128)S(6)} %select_n.182, s32[]{:T(128)} %constant.327.clone, s32[]{:T(128)} %constant.327.clone, s32[]{:T(128)} %constant.327.clone) | dynamic-update-slice | bytes 8388612 | tf_op jit(solution)/shard_map/while/body/eval_jaxpr/cond/branch_1_fun/dynamic_update_slice | solution.py:78
  912.0 406.9 %psum.7 = f32[32]{0:T(128)S(1)} all-reduce(f32[32]{0:T(128)S(1)} %multiply_dynamic-update-slice_fusion), channel_id=1, replica_groups=mesh['dp'=2,'head'=2,'ctx'=8] {'dp','head','ctx'}, use_global_device_ids=true, to_apply=%region_20.21 | all-reduce | flops 32 | bytes 256 | tf_op jit(solution)/shard_map/psum | solution.py:197
  (383 shorter events, 356.3 us)
Async XLA Ops:
  7.2 14.1 %copy-start.11 = (f32[16]{0:T(128)S(1)}, f32[16]{0:T(128)}, u32[]{:S(2)}) copy-start(f32[16]{0:T(128)} %param.21) | copy-start | bytes 196
  7.2 14.1 %copy-start.9 = (s32[16]{0:T(128)S(1)}, s32[16]{0:T(128)}, u32[]{:S(2)}) copy-start(s32[16]{0:T(128)} %param.22) | copy-start | bytes 196
  7.2 300.0 %all-gather.2.cloned.1.call-start = ((), (), s32[]{:S(2)}) async-start(), calls=%async_computation | async-start | bytes 18874368 | tf_op jit(solution)/shard_map/all_gather | solution.py:141
  10.1 1.4 copy-start
  11.6 72.5 %collective-permute-start.1 = (bf16[2,1024,4,128]{3,1,2,0:T(8,128)(2,1)}, bf16[2,1024,4,128]{3,1,2,0:T(8,128)(2,1)}, u32[]{:S(2)}, u32[]{:S(2)}) collective-permute-start(bf16[2,1024,4,128]{3,1,2,0:T(8,128)(2,1)} %copy-done), channel_id=1, source_target_pairs={{0,1},{1,2},{2,3},{3,4},{4,5},{5,6},{6,7},{8,9},{9,10},{10,11},{11... | collective-permute-start | bytes 6291464 | tf_op jit(solution)/shard_map/ppermute | solution.py:16
  17.8 88.1 %collective-permute-start = (bf16[2,1024,4,128]{3,1,2,0:T(8,128)(2,1)}, bf16[2,1024,4,128]{3,1,2,0:T(8,128)(2,1)}, u32[]{:S(2)}, u32[]{:S(2)}) collective-permute-start(bf16[2,1024,4,128]{3,1,2,0:T(8,128)(2,1)} %copy-done), channel_id=1, source_target_pairs={{0,2},{1,3},{2,4},{3,5},{4,6},{5,7},{8,10},{9,11},{10,12},{11,13},... | collective-permute-start | bytes 6291464 | tf_op jit(solution)/shard_map/ppermute | solution.py:16
  21.3 14.1 %copy-start.4 = (f32[4,4]{1,0:T(4,128)}, f32[4,4]{1,0:T(4,128)S(1)}, u32[]{:S(2)}) copy-start(f32[4,4]{1,0:T(4,128)S(1)} %mul.157) | copy-start | bytes 196
  42.1 63.8 %copy-start.1 = (bf16[2,1024,4,128]{3,1,2,0:T(8,128)(2,1)S(1)}, bf16[2,1024,4,128]{3,1,2,0:T(8,128)(2,1)}, u32[]{:S(2)}) copy-start(bf16[2,1024,4,128]{3,1,2,0:T(8,128)(2,1)} %copy-done) | copy-start | bytes 6291460
  450.3 5.1 copy-start.2
  467.1 433.6 %copy-start.3 = (f32[1024,4,1]{0,1,2:T(4,128)S(1)}, f32[1024,4,1]{0,1,2:T(4,128)}, u32[]{:S(2)}) copy-start(f32[1024,4,1]{0,1,2:T(4,128)} %copy-done.2) | copy-start | bytes 49156
  900.8 2.0 copy-start.5
  900.8 2.0 copy-start.6
  900.8 2.0 copy-start.7
  900.8 2.0 copy-start.8
  902.8 9.1 copy-start.10
Sparse Core Ops, SparseCore 0:
  11.7 295.4 all-gather.1
where the time goes:
time: 1350 us; the launch traced here: 1330 us
  blocking collectives  407 us (30%)
  local copies, waits for them, and re-layouts  345 us (26%)
  waiting for transfers between devices  254 us (19%)
  matrix products  163 us (12%)
  loops' own time  74.7 us (6%)
  other arithmetic  66.5 us (5%)
  between operations  14.2 us (1%)
    psum x1, blocking collectives, on_device(): totals = lax.psum(padded, ('dp', 'head', 'ctx'))  407 us
    dynamic_update_slice x39, local copies, waits for them, and re-layouts, compute(): lax.dynamic_update_slice_in_dim(member, fresh_part, row_at, 0)  222 us
    all_gather x1, waiting for transfers between devices, on_device(): portion = lax.all_gather(stacked, 'ctx', axis=1, tiled=True)  190 us
    dot_general x13, matrix products, block_update(): jnp.einsum('rgek,kgh->rgeh', weights.astype(jnp.bfloat16), value_rows, pr...  101 us
    another operation x3, loops' own time, sweep_blocks(): return lax.fori_loop(0, total_steps, visit_block, carried)  73.2 us
    ppermute x2, waiting for transfers between devices, from_behind(): return lax.ppermute(block, axis, route)  63.6 us
    dot_general x13, matrix products, block_update(): jnp.einsum('rgeh,kgh->rgek', query_block, key_rows, preferred_element_typ...  56.9 us
    reduce_sum x13, other arithmetic, block_update(): running_sum = running_sum * factor + jnp.sum(weights, axis=-1)  43.3 us
  transfers between devices with their start and end apart: 3, of which 3 were waited for; matrix products, arithmetic and copies ran while one was open for 2% of the time, Pallas kernels for 0%

commit v1 on v0

v1 whole, which is shorter than its diff:
```python
import functools
import math

import jax
import jax.numpy as jnp
from jax import lax
from jax.experimental import pallas as pl
from jax.experimental.pallas import tpu as pltpu
from jax.sharding import PartitionSpec as P

SINK = 64
WINDOW = 2048
BLOCK = 512
LANES = 128
NT = (((1,), (1,)), ((), ()))


def lane_sum(weights):
    total = weights[:, :LANES]
    for at in range(LANES, weights.shape[1], LANES):
        total = total + weights[:, at : at + LANES]
    return total


def update(m_ref, l_ref, acc_ref, query, keys, values, factor, mask, first=False):
    scores = lax.dot_general(query, keys, NT, preferred_element_type=jnp.float32)
    if mask is not None:
        scores = jnp.where(mask, scores, -jnp.inf)
    highest = jnp.max(scores, axis=1, keepdims=True)
    if not first:
        before = m_ref[:, :1]
        highest = jnp.maximum(before, highest)
    weights = jnp.exp2((scores - highest) * factor)
    part = jnp.dot(weights.astype(jnp.bfloat16), values, preferred_element_type=jnp.float32)
    sums = lane_sum(weights)
    if first:
        l_ref[...] = sums
        acc_ref[...] = part
    else:
        shrink = jnp.exp2((before - highest) * factor)
        l_ref[...] = l_ref[...] * shrink + sums
        acc_ref[...] = acc_ref[...] * shrink + part
    m_ref[...] = jnp.broadcast_to(highest, m_ref.shape)


def grid_of(rows, cols):
    shape = (rows, cols)
    return lax.broadcasted_iota(jnp.int32, shape, 0), lax.broadcasted_iota(jnp.int32, shape, 1)


def near_kernel(per_group, factor, meta, q, k, v, sk, sv, out, om, ol, oacc, m, l, acc):
    group, qb = pl.program_id(0), pl.program_id(1)
    back = WINDOW // BLOCK
    first_row = meta[0] + qb * BLOCK
    heads = range(per_group)

    def visit(block, mask, first=False):
        rows = pl.ds(pl.multiple_of(block * BLOCK, BLOCK), BLOCK)
        keys, values = k[rows, :], v[rows, :]
        for e in heads:
            query = q[:, e * LANES : (e + 1) * LANES]
            update(m.at[e], l.at[e], acc.at[e], query, keys, values, factor, mask, first)

    row, col = grid_of(BLOCK, BLOCK)
    visit(qb + back, col <= row, True)

    def middle(block, _):
        visit(block, None)
        return 0

    valid_from = back - meta[0] // BLOCK
    lax.fori_loop(jnp.maximum(qb + 1, valid_from), qb + back, middle, 0)

    @pl.when(first_row >= WINDOW)
    def _():
        row2, col2 = grid_of(BLOCK, BLOCK)
        visit(qb, col2 > row2)
        srow, scol = grid_of(BLOCK, LANES)
        seen = (scol < SINK) & (scol <= srow + first_row - WINDOW)
        for e in heads:
            query = q[:, e * LANES : (e + 1) * LANES]
            update(m.at[e], l.at[e], acc.at[e], query, sk[...], sv[...], factor, seen)

    for e in heads:
        total = jnp.sum(l[e], axis=1, keepdims=True)
        out[:, e * LANES : (e + 1) * LANES] = (acc[e] / total).astype(jnp.bfloat16)

    slot = meta[1 + group]
    om[0] = m[slot]
    ol[0] = l[slot]
    oacc[0] = acc[slot]


def far_kernel(groups, factor, meta, gates, q, k, v, og, m0, l0, a0, base, out, grad, m, l, acc):
    del base
    group, qb = pl.program_id(0), pl.program_id(1)
    first_row = meta[0] + qb * BLOCK
    m[...] = m0[0]
    l[...] = l0[0]
    acc[...] = a0[0]

    def visit(block, mask):
        rows = pl.ds(pl.multiple_of(block * BLOCK, BLOCK), BLOCK)
        update(m, l, acc, q[...], k[rows, :], v[rows, :], factor, mask)

    last = (first_row - WINDOW) // BLOCK

    @pl.when(first_row >= WINDOW)
    def _():
        row, col = grid_of(BLOCK, BLOCK)
        visit(last, (col <= row) & (col + last * BLOCK >= SINK))

    @pl.when(first_row > WINDOW)
    def _():
        _, col = grid_of(BLOCK, BLOCK)
        visit(0, col >= SINK)

    def middle(block, _):
        visit(block, None)
        return 0

    lax.fori_loop(1, last, middle, 0)
    near = a0[0] / jnp.sum(l0[0], axis=1, keepdims=True)
    full = acc[...] / jnp.sum(l[...], axis=1, keepdims=True)
    gate = gates[group]
    out[...] = (gate * full + (1.0 - gate) * near).astype(jnp.bfloat16)
    terms = og[...].astype(jnp.float32) * (full - near)
    grad[0, 0] = jnp.sum(terms.reshape(BLOCK // 8, 8, LANES), axis=0)


def from_behind(block, axis, distance):
    devices = range(lax.axis_size(axis))
    route = [(i - distance, i) for i in devices if i - distance in devices]
    return lax.ppermute(block, axis, route)


def on_device(query_states, key_states, value_states, gate_values, head_flags, output_grad):
    tok = query_states.shape[1]
    groups, width = key_states.shape[2], key_states.shape[3]
    heads = query_states.shape[2]
    per = heads // groups
    ctx_count = lax.axis_size("ctx")
    seq = tok * ctx_count
    depth = WINDOW // tok
    factor = math.log2(math.e) / math.sqrt(width)
    queries = query_states.reshape(tok, heads * width)
    grads = output_grad.reshape(tok, heads * width)
    kv = jnp.concatenate(
        [key_states.reshape(tok, groups * width), value_states.reshape(tok, groups * width)], axis=1
    )
    earlier = [from_behind(kv, "ctx", d) for d in range(depth, 0, -1)]
    near_kv = jnp.concatenate(earlier + [kv], axis=0)
    sinks = lax.all_gather(kv[:SINK], "ctx", axis=0)[0]
    sinks = jnp.pad(sinks, ((0, LANES - SINK), (0, 0)))
    all_kv = lax.all_gather(kv, "ctx", axis=0, tiled=True)

    marked = head_flags.reshape(groups, per)
    slots = jnp.argmax(marked, axis=1).astype(jnp.int32)
    start = (lax.axis_index("ctx") * tok).astype(jnp.int32)
    meta = jnp.concatenate([start[None], slots])
    gates = jnp.sum(gate_values.reshape(groups, per) * marked.astype(jnp.float32), axis=1)
    qblocks = tok // BLOCK
    grid = (groups, qblocks)
    state = jax.ShapeDtypeStruct((groups, tok, LANES), jnp.float32)
    state_spec = pl.BlockSpec((1, BLOCK, LANES), lambda g, i, *_: (g, i, 0))
    span = near_kv.shape[0]
    params = pltpu.CompilerParams(vmem_limit_bytes=40 * 1024 * 1024)

    near_pairs = heads * tok * (WINDOW + BLOCK)
    near_out, m0, l0, a0 = pl.pallas_call(
        functools.partial(near_kernel, per, factor),
        grid_spec=pltpu.PrefetchScalarGridSpec(
            num_scalar_prefetch=1,
            grid=grid,
            in_specs=[
                pl.BlockSpec((BLOCK, per * width), lambda g, i, *_: (i, g)),
                pl.BlockSpec((span, width), lambda g, i, *_: (0, g)),
                pl.BlockSpec((span, width), lambda g, i, *_: (0, groups + g)),
                pl.BlockSpec((LANES, width), lambda g, i, *_: (0, g)),
                pl.BlockSpec((LANES, width), lambda g, i, *_: (0, groups + g)),
            ],
            out_specs=[
                pl.BlockSpec((BLOCK, per * width), lambda g, i, *_: (i, g)),
                state_spec,
                state_spec,
                state_spec,
            ],
            scratch_shapes=[pltpu.VMEM((per, BLOCK, LANES), jnp.float32)] * 3,
        ),
        out_shape=[jax.ShapeDtypeStruct((tok, heads * width), jnp.bfloat16), state, state, state],
        compiler_params=params,
        cost_estimate=pl.CostEstimate(
            flops=4 * near_pairs * width, bytes_accessed=32 << 20, transcendentals=near_pairs
        ),
        name="near",
    )(meta, queries, near_kv, near_kv, sinks, sinks)

    far_pairs = groups * tok * seq
    mine = pl.BlockSpec((BLOCK, width), lambda g, i, meta, *_: (i, g * per + meta[1 + g]))
    blended, partial = pl.pallas_call(
        functools.partial(far_kernel, groups, factor),
        grid_spec=pltpu.PrefetchScalarGridSpec(
            num_scalar_prefetch=2,
            grid=grid,
            in_specs=[
                mine,
                pl.BlockSpec((seq, width), lambda g, i, *_: (0, g)),
                pl.BlockSpec((seq, width), lambda g, i, *_: (0, groups + g)),
                mine,
                state_spec,
                state_spec,
                state_spec,
                pl.BlockSpec(memory_space=pl.ANY),
            ],
            out_specs=[
                mine,
                pl.BlockSpec((1, 1, 8, LANES), lambda g, i, *_: (g, i, 0, 0)),
            ],
            scratch_shapes=[pltpu.VMEM((BLOCK, LANES), jnp.float32)] * 3,
        ),
        out_shape=[
            jax.ShapeDtypeStruct((tok, heads * width), jnp.bfloat16),
            jax.ShapeDtypeStruct((groups, qblocks, 8, LANES), jnp.float32),
        ],
        input_output_aliases={9: 0},
        compiler_params=params,
        cost_estimate=pl.CostEstimate(
            flops=2 * far_pairs * width, bytes_accessed=32 << 20, transcendentals=far_pairs // 2
        ),
        name="far",
    )(meta, gates, queries, all_kv, all_kv, grads, m0, l0, a0, near_out)

    local = (jnp.sum(partial, axis=(1, 2, 3))[:, None] * marked.astype(jnp.float32)).reshape(heads)
    padded = lax.dynamic_update_slice_in_dim(
        jnp.zeros((heads * lax.axis_size("head"),), jnp.float32),
        local,
        lax.axis_index("head") * heads,
        0,
    )
    totals = lax.psum(padded, ("dp", "head", "ctx"))
    count = lax.axis_size("dp") * query_states.shape[0] * seq * width
    return blended.reshape(1, tok, heads, width), totals * (1.0 / math.sqrt(count))


def solution(mesh):
    return jax.shard_map(
        on_device,
        mesh=mesh,
        in_specs=(
            P("dp", "ctx", "head", None),
            P("dp", "ctx", "head", None),
            P("dp", "ctx", "head", None),
            P("head"),
            P("head"),
            P("dp", "ctx", "head", None),
        ),
        out_specs=(P("dp", "ctx", "head", None), P()),
        check_vma=False,
    )
```

time: 1350 us -> 492 us (0.36); the launches traced: 1330 us -> 491 us
  local copies, waits for them, and re-layouts: 345 us -> 34.8 us
  blocking collectives: 407 us -> 125 us
  matrix products: 163 us -> 0 us
  loops' own time: 74.7 us -> 0 us
  other arithmetic: 66.5 us -> 8.01 us
  Pallas kernels: 0 us -> 43.7 us
    psum x1, blocking collectives: 407 us -> 125 us  [on_device(): totals = lax.psum(padded, ('dp', 'head', 'ctx'))]
    dynamic_update_slice x39 -> x0, local copies, waits for them, and re-layouts: 222 us -> none  [compute(): lax.dynamic_update_slice_in_dim(member, fresh_part, row_at, 0)]
    dot_general x27 -> x0, matrix products: 163 us -> none  [the longest x13 101 us: block_update(): jnp.einsum('rgek,kgh->rgeh', weights.astype(jnp.bfloat16), value_rows, pr...]
    another operation x49 -> x0, loops' own time: 74.7 us -> none  [the longest x3 73.2 us: sweep_blocks(): return lax.fori_loop(0, total_steps, visit_block, carried)]
    reduce_sum x14 -> x2, other arithmetic: 52.3 us -> 0.23 us  [the longest x1 0.12 us: on_device(): jnp.sum(gate_values.reshape(groups, per) * marked.astype(jnp.float32), ax...]
    slice x78 -> x1, local copies, waits for them, and re-layouts: 46.6 us -> 0.74 us  [on_device(): sinks = lax.all_gather(kv[:SINK], 'ctx', axis=0)[0]]
    ppermute x2, waiting for transfers between devices: 63.6 us -> 18.4 us  [from_behind(): return lax.ppermute(block, axis, route)]
    all_gather x1 -> x2, waiting for transfers between devices: 190 us -> 236 us  [the longest x1 215 us: on_device(): all_kv = lax.all_gather(kv, 'ctx', axis=0, tiled=True)]
  transfers between devices with their start and end apart: 3 -> 4, of which waited for: 3 -> 3; matrix products, arithmetic and copies ran while one was open for 2% -> 4% of each run, Pallas kernels for 0% -> 7%
where the time goes in v1:
time: 492 us; the launch traced here: 491 us
  waiting for transfers between devices  254 us (52%)
  blocking collectives  125 us (25%)
  Pallas kernels  43.7 us (9%)
  local copies, waits for them, and re-layouts  34.8 us (7%)
  between operations  14.1 us (3%)
  starting transfers between devices  11.1 us (2%)
  other arithmetic  8.01 us (2%)
    all_gather x1, waiting for transfers between devices, on_device(): all_kv = lax.all_gather(kv, 'ctx', axis=0, tiled=True)  215 us
    psum x1, blocking collectives, on_device(): totals = lax.psum(padded, ('dp', 'head', 'ctx'))  125 us
    unnamed x28, local copies, waits for them, and re-layouts  32.3 us
    pallas_call x1, Pallas kernels, on_device(): pl.pallas_call(functools.partial(near_kernel, per, factor), grid_spec=plt...  32.3 us
    all_gather x1, waiting for transfers between devices, on_device(): sinks = lax.all_gather(kv[:SINK], 'ctx', axis=0)[0]  20.7 us
    ppermute x2, waiting for transfers between devices, from_behind(): return lax.ppermute(block, axis, route)  18.4 us
    pallas_call x1, Pallas kernels, on_device(): pl.pallas_call(functools.partial(far_kernel, groups, factor), grid_spec=p...  11.5 us
    ppermute x2, starting transfers between devices, from_behind(): return lax.ppermute(block, axis, route)  11 us
  transfers between devices with their start and end apart: 4, of which 3 were waited for; matrix products, arithmetic and copies ran while one was open for 4% of the time, Pallas kernels for 7%

profile of v1, /device:TPU:0, one launch (start us, length us, event | category | flops | bytes accessed | tf_op | source)
XLA Modules:
  0.0 491.2 jit_solution(15122336804127618205)
XLA Ops:
  7.2 1.4 bitcast_dynamic-update-slice_fusion.1
  8.6 1.4 bitcast_dynamic-update-slice_fusion
  10.1 0.7 slice.10
  10.9 0.5 copy-done.7
  11.4 0.2 all-gather.4.cloned.1.call-update
  11.6 6.3 %collective-permute-start = (bf16[1024,1024]{1,0:T(8,128)(2,1)}, bf16[1024,1024]{1,0:T(8,128)(2,1)}, u32[]{:S(2)}, u32[]{:S(2)}) collective-permute-start(bf16[1024,1024]{1,0:T(8,128)(2,1)} %copy-done.7), channel_id=1, source_target_pairs={{0,2},{1,3},{2,4},{3,5},{4,6},{5,7},{8,10},{9,11},{10,12},{11,13},... | collective-permute-start | bytes 6291464 | tf_op jit(solution)/shard_map/ppermute | solution.py:134
  17.9 4.8 collective-permute-start.1
  22.6 0.1 reshape.28
  22.7 6.3 %copy.19 = bf16[128,8,16,128]{3,1,2,0:T(8,128)(2,1)} copy(bf16[128,8,16,128]{3,2,1,0:T(8,128)(2,1)} %bitcast.26) | data formatting | bytes 8388608
  29.1 6.5 %copy.18 = bf16[128,8,16,128]{3,1,2,0:T(8,128)(2,1)} copy(bf16[128,8,16,128]{3,2,1,0:T(8,128)(2,1)} %bitcast.27) | data formatting | bytes 8388608
  35.6 0.6 iota_reduce_fusion
  36.3 0.1 multiply_reduce_fusion.gates
  36.5 20.7 %all-gather.6.cloned.1.call-done = bf16[512,1024]{1,0:T(8,128)(2,1)} async-done(((bf16[64,1024]{1,0:T(8,128)(2,1)}), bf16[512,1024]{1,0:T(8,128)(2,1)}) %all-gather.6.cloned.1.call-update) | async-done | bytes 1048592 | tf_op jit(solution)/shard_map/all_gather | solution.py:153
  57.1 1.0 slice_select_fusion.sk.sv
  58.2 18.4 %collective-permute-done = bf16[1024,1024]{1,0:T(8,128)(2,1)} collective-permute-done((bf16[1024,1024]{1,0:T(8,128)(2,1)}, bf16[1024,1024]{1,0:T(8,128)(2,1)}, u32[]{:S(2)}, u32[]{:S(2)}) %collective-permute-start) | collective-permute-done | bytes 2097184 | tf_op jit(solution)/shard_map/ppermute | solution.py:134
  76.5 5.4 %pad_maximum_fusion.k.v = bf16[3072,1024]{1,0:T(8,128)(2,1)} fusion(bf16[1024,1024]{1,0:T(8,128)(2,1)S(1)} %copy-done.8, bf16[1024,1024]{1,0:T(8,128)(2,1)} %collective-permute-done.1, bf16[1024,1024]{1,0:T(8,128)(2,1)} %collective-permute-done), kind=kLoop, calls=%fused_computation | loop fusion | flops 18874368 | bytes 12582912 | tf_op jit(solution)/shard_map/concatenate | solution.py:152
  82.0 32.3 %near.1 = (bf16[1024,2048]{1,0:T(8,128)(2,1)S(1)}, f32[4,1024,128]{2,1,0:T(8,128)S(1)}, f32[4,1024,128]{2,1,0:T(8,128)S(1)}, f32[4,1024,128]{2,1,0:T(8,128)S(1)}) custom-call(s32[5]{0:T(128)S(1)} %pad_add_fusion.meta, bf16[1024,2048]{1,0:T(8,128)(2,1)} %bitcast.23, bf16[3072,1024]{1,0:T(8,128)(2,1)} %pad_maximum_fusion.k.v, ...), custom_call_target="tpu_custom_call" | custom-call | flops 21474836480 | bytes 33554432 | tf_op jit(solution)/shard_map/near/pallas_call | solution.py:170
  114.3 1.9 copy-done
  116.2 1.3 copy-done.3
  117.5 1.3 copy-done.5
  118.8 214.9 %all-gather.4.cloned.1.call-done.k.v = bf16[8192,1024]{1,0:T(8,128)(2,1)} async-done(((bf16[1024,1024]{1,0:T(8,128)(2,1)}), bf16[8192,1024]{1,0:T(8,128)(2,1)}) %all-gather.4.cloned.1.call-update) | async-done | bytes 16777232 | tf_op jit(solution)/shard_map/all_gather | solution.py:155
  333.7 2.2 copy-done.1
  335.9 1.6 copy-done.4
  337.5 1.6 copy-done.6
  339.1 11.5 %far.1 = (bf16[1024,2048]{1,0:T(8,128)(2,1)S(1)}, f32[4,2,8,128]{3,2,1,0:T(8,128)S(1)}) custom-call(s32[5]{0:T(128)S(1)} %pad_add_fusion.meta, f32[4]{0:T(128)S(1)} %multiply_reduce_fusion.gates, bf16[1024,2048]{1,0:T(8,128)(2,1)} %bitcast.24, bf16[8192,1024]{1,0:T(8,128)(2,1)} %all-gather.4.cloned.1.call-done.k.v, ...), custom_call_target="tpu_custom_call", output_to_operand_aliasing={{0}: (9, {})} | custom-call | flops 8589934592 | bytes 33554432 | tf_op jit(solution)/shard_map/far/pallas_call | solution.py:200
  350.5 1.9 copy-done.2
  352.5 0.1 reduce_sum.19
  352.7 0.1 mul.29
  352.7 0.1 multiply_dynamic-update-slice_fusion
  352.8 5.6 %copy.13 = bf16[128,8,16,128]{3,2,1,0:T(8,128)(2,1)} copy(bf16[128,8,16,128]{3,1,2,0:T(8,128)(2,1)} %bitcast.22) | data formatting | bytes 8388608
  358.5 125.4 %psum.7 = f32[32]{0:T(128)S(1)} all-reduce(f32[32]{0:T(128)S(1)} %multiply_dynamic-update-slice_fusion), channel_id=1, replica_groups=mesh['dp'=2,'head'=2,'ctx'=8] {'dp','head','ctx'}, use_global_device_ids=true, to_apply=%region_3.4 | all-reduce | flops 32 | bytes 256 | tf_op jit(solution)/shard_map/psum | solution.py:240
  483.9 0.5 broadcast_multiply_fusion
  (24 shorter events, 0.4 us)
Async XLA Ops:
  7.2 15.5 %copy-start.9 = (s32[16]{0:T(128)S(1)}, s32[16]{0:T(128)}, u32[]{:S(2)}) copy-start(s32[16]{0:T(128)} %param.10) | copy-start | bytes 196
  7.2 50.0 %all-gather.6.cloned.1.call-start = ((), (), s32[]{:S(2)}) async-start(), calls=%async_computation.1 | async-start | bytes 1179648 | tf_op jit(solution)/shard_map/all_gather | solution.py:153
  10.1 1.3 copy-start.7
  10.8 322.9 %all-gather.4.cloned.1.call-start = ((), (), s32[]{:S(2)}) async-start(), calls=%async_computation | async-start | bytes 18874368 | tf_op jit(solution)/shard_map/all_gather | solution.py:155
  11.6 64.9 %collective-permute-start = (bf16[1024,1024]{1,0:T(8,128)(2,1)}, bf16[1024,1024]{1,0:T(8,128)(2,1)}, u32[]{:S(2)}, u32[]{:S(2)}) collective-permute-start(bf16[1024,1024]{1,0:T(8,128)(2,1)} %copy-done.7), channel_id=1, source_target_pairs={{0,2},{1,3},{2,4},{3,5},{4,6},{5,7},{8,10},{9,11},{10,12},{11,13},... | collective-permute-start | bytes 6291464 | tf_op jit(solution)/shard_map/ppermute | solution.py:134
  17.9 58.7 %collective-permute-start.1 = (bf16[1024,1024]{1,0:T(8,128)(2,1)}, bf16[1024,1024]{1,0:T(8,128)(2,1)}, u32[]{:S(2)}, u32[]{:S(2)}) collective-permute-start(bf16[1024,1024]{1,0:T(8,128)(2,1)} %copy-done.7), channel_id=1, source_target_pairs={{0,1},{1,2},{2,3},{3,4},{4,5},{5,6},{6,7},{8,9},{9,10},{10,11},{11... | collective-permute-start | bytes 6291464 | tf_op jit(solution)/shard_map/ppermute | solution.py:134
  22.7 6.3 %copy-start.11 = (f32[16]{0:T(128)S(1)}, f32[16]{0:T(128)}, u32[]{:S(2)}) copy-start(f32[16]{0:T(128)} %param.9) | copy-start | bytes 196
  29.1 28.0 %copy-start.10 = (pred[128]{0:T(512)(128)(4,1)S(1)}, pred[128]{0:T(512)(128)(4,1)}, u32[]{:S(2)}) copy-start(pred[128]{0:T(512)(128)(4,1)} %constant.35) | copy-start | bytes 388
  29.1 47.4 %copy-start.8 = (bf16[1024,1024]{1,0:T(8,128)(2,1)S(1)}, bf16[1024,1024]{1,0:T(8,128)(2,1)}, u32[]{:S(2)}) copy-start(bf16[1024,1024]{1,0:T(8,128)(2,1)} %copy-done.7) | copy-start | bytes 6291460
  114.3 1.9 copy-start
  116.2 1.3 copy-start.3
  117.5 1.3 copy-start.5
  333.7 2.2 copy-start.1
  335.9 1.6 copy-start.4
  337.5 1.6 copy-start.6
  350.5 1.9 copy-start.2
Sparse Core Ops, SparseCore 0:
  11.0 46.1 all-gather.5
  59.3 274.3 all-gather.3
